TPU v7x, 32 devices: a whole 2x2x4 slice. The times are simulated.
32 devices in a mesh: section: 2 (over x), dp: 4 (over z), mp: 4 (over y, core).
Axes of the slice: x: 2, y: 2, z: 4, core: 2. Of those that a mesh axis runs over, the one named last changes fastest.
Arguments:
- activations: bfloat16 [2, 64, 12288], P('section', 'dp', 'mp'), may hold values from -50 to 50, as said below
- norm_gain: bfloat16 [2, 12288], P('section', 'mp'), may hold values from 0.25 to 1.75
- norm_shift: bfloat16 [2, 12288], P('section', 'mp'), may hold values from -3 to 3
- up_weight: bfloat16 [2, 12288, 49152], P('section', 'mp', 'dp'), may hold values from -0.0546875 to 0.0546875
- up_bias: bfloat16 [2, 49152], P('section', 'dp'), may hold values from -3 to 3
Outputs:
- hidden: bfloat16 [2, 64, 49152], P('section', 'mp', 'dp')
Inputs may be any that keep to these rules, and one draw needn't show every extreme that they name: Real-valued activations.
All inputs are finite; a program needn't handle non-finite values.
Results may differ from a plain program's by a relative error of at most 0.014.
Values may be sent and summed in bfloat16 or wider, within the bound.
No kernel may reach another device: no remote copies, remote signals or barrier semaphores. Data moves between devices by JAX's collectives and lax.ppermute only.
A program may use at most 128 MiB of HBM per device.

v0:
```python
import jax
import jax.numpy as jnp
from jax import lax
from jax.sharding import PartitionSpec as P

D = 12288


def shifted(value, axis, by):
    devices = lax.axis_size(axis)
    return lax.ppermute(value, axis, [(i, (i + by) % devices) for i in range(devices)])


def normalize(block, gain, shift):
    values = block.astype(jnp.float32)
    first_sum, second_sum = lax.psum(
        (jnp.sum(values, axis=1), jnp.sum(values * values, axis=1)), "mp"
    )
    average = (first_sum / D)[:, None]
    moment = (second_sum / D)[:, None]
    scaled = (values - average) * lax.rsqrt(moment - average * average + 1e-05)
    return (scaled * gain + shift).astype(jnp.bfloat16)


def body(activations, norm_gain, norm_shift, up_weight, up_bias):
    weight = up_weight[0]
    gain = norm_gain[0].astype(jnp.float32)
    shift = norm_shift[0].astype(jnp.float32)
    bias = up_bias[0].astype(jnp.float32)
    received = shifted(activations[0], "section", 1)
    normed_block = normalize(received, gain, shift)
    normed = lax.all_gather(normed_block, "dp", axis=0, tiled=True)
    total = lax.psum_scatter(
        jnp.dot(normed, weight, preferred_element_type=jnp.float32).astype(jnp.bfloat16),
        "mp",
        scatter_dimension=0,
        tiled=True,
    ).astype(jnp.float32)
    result = jax.nn.gelu(total + bias, approximate=True).astype(jnp.bfloat16)
    return result[None]


def solution(mesh):
    in_specs = (
        P("section", "dp", "mp"),
        P("section", "mp"),
        P("section", "mp"),
        P("section", "mp", "dp"),
        P("section", "dp"),
    )
    out_specs = P("section", "mp", "dp")
    return jax.shard_map(body, mesh=mesh, in_specs=in_specs, out_specs=out_specs, check_vma=False)
```

profile of v0, /device:TPU:0, one launch (start us, length us, event | category | flops | bytes accessed | tf_op | source)
XLA Modules:
  0.0 101.3 jit_solution(6768804129994490177)
XLA Ops:
  6.5 0.0 copy-start
  6.5 0.0 reduce-scatter.2.cloned.1.call-start
  6.5 2.9 %collective-permute-start = (bf16[16,3072]{1,0:T(8,128)(2,1)}, bf16[16,3072]{1,0:T(8,128)(2,1)S(1)}, u32[]{:S(2)}, u32[]{:S(2)}) collective-permute-start(bf16[16,3072]{1,0:T(8,128)(2,1)} %bitcast.15), channel_id=1, source_target_pairs={{0,16},{16,0},{1,17},{17,1},{2,18},{18,2},{3,19},{19,3},{4,20},{20... | collective-permute-start | bytes 294920 | tf_op jit(solution)/shard_map/ppermute | solution.py:11
  9.5 0.7 mul.64
  10.2 0.7 add.57
  10.9 1.6 %collective-permute-done = bf16[16,3072]{1,0:T(8,128)(2,1)S(1)} collective-permute-done((bf16[16,3072]{1,0:T(8,128)(2,1)}, bf16[16,3072]{1,0:T(8,128)(2,1)S(1)}, u32[]{:S(2)}, u32[]{:S(2)}) %collective-permute-start) | collective-permute-done | bytes 98336 | tf_op jit(solution)/shard_map/ppermute | solution.py:11
  12.5 0.1 convert_reduce_fusion
  12.6 5.8 %all-reduce = (f32[16]{0:T(128)S(1)}, f32[16]{0:T(128)S(1)}) all-reduce(f32[16]{0:T(128)S(1)} %get-tuple-element.6, f32[16]{0:T(128)S(1)} %get-tuple-element.5), channel_id=1, replica_groups=mesh['section'=2,'dp'=4,'mp'=4] {'mp'}, use_global_device_ids=true, to_apply=%region_3.0 | all-reduce | flops 32 | bytes 256 | tf_op jit(solution)/shard_map/psum | solution.py:16
  18.4 0.1 fusion.17
  18.5 15.0 %all_gather.3 = bf16[64,3072]{1,0:T(8,128)(2,1)S(1)} all-gather(bf16[16,3072]{1,0:T(8,128)(2,1)S(1)} %fusion.17), channel_id=1, replica_groups=mesh['section'=2,'dp'=4,'mp'=4] {'dp'}, dimensions={0}, use_global_device_ids=true | all-gather | bytes 491520 | tf_op jit(solution)/shard_map/all_gather | solution.py:32
  33.5 28.5 %fusion.2 = bf16[64,12288]{1,0:T(8,128)(2,1)} fusion(bf16[64,3072]{1,0:T(8,128)(2,1)S(1)} %all_gather.3, bf16[1,3072,12288]{2,1,0:T(8,128)(2,1)} %param.8), kind=kOutput, calls=%fused_computation.2 | convolution fusion | flops 4832624640 | bytes 77463552 | tf_op jit(solution)/shard_map/dot_general | solution.py:34
  62.0 0.0 reduce-scatter.2.cloned.1.call-update
  62.0 0.0 copy-done
  62.0 0.1 add.58
  62.1 30.3 %reduce-scatter.2.cloned.1.call-done = bf16[16,12288]{1,0:T(8,128)(2,1)} async-done(((bf16[64,12288]{1,0:T(8,128)(2,1)}), bf16[16,12288]{1,0:T(8,128)(2,1)}) %reduce-scatter.2.cloned.1.call-update) | async-done | bytes 393232 | tf_op jit(solution)/shard_map/reduce_scatter | solution.py:33
  92.4 2.0 %fusion.13 = bf16[1,16,12288]{2,1,0:T(8,128)(2,1)} fusion(bf16[16,12288]{1,0:T(8,128)(2,1)} %reduce-scatter.2.cloned.1.call-done, f32[12288]{0:T(1024)S(1)} %bitcast.12), kind=kLoop, calls=%fused_computation.12 | loop fusion | flops 2162688 | bytes 835584 | tf_op jit(solution)/shard_map/broadcast_in_dim | solution.py:40
  (1 shorter events, 0.0 us)
Async XLA Ops:
  6.5 55.5 %copy-start = (bf16[1,12288]{1,0:T(2,128)(2,1)S(1)}, bf16[1,12288]{1,0:T(2,128)(2,1)}, u32[]{:S(2)}) copy-start(bf16[1,12288]{1,0:T(2,128)(2,1)} %param.9) | copy-start | bytes 73732
  6.5 85.9 %reduce-scatter.2.cloned.1.call-start = ((), (), s32[]{:S(2)}) async-start(), calls=%async_computation.1 | async-start | bytes 1966080 | tf_op jit(solution)/shard_map/reduce_scatter | solution.py:33
  6.5 5.9 %collective-permute-start = (bf16[16,3072]{1,0:T(8,128)(2,1)}, bf16[16,3072]{1,0:T(8,128)(2,1)S(1)}, u32[]{:S(2)}, u32[]{:S(2)}) collective-permute-start(bf16[16,3072]{1,0:T(8,128)(2,1)} %bitcast.15), channel_id=1, source_target_pairs={{0,16},{16,0},{1,17},{17,1},{2,18},{18,2},{3,19},{19,3},{4,20},{20... | collective-permute-start | bytes 294920 | tf_op jit(solution)/shard_map/ppermute | solution.py:11
Sparse Core Ops, SparseCore 0:
  62.2 30.2 reduce-scatter.1
where the time goes:
time: 102 us; the launch traced here: 101 us
  waiting for transfers between devices  31.9 us (31%)
  matrix products  28.5 us (28%)
  blocking collectives  20.8 us (20%)
  between operations  13.4 us (13%)
  other arithmetic  3.8 us (4%)
  starting transfers between devices  2.94 us (3%)
    reduce_scatter x1, waiting for transfers between devices, body(): lax.psum_scatter(jnp.dot(normed, weight, preferred_element_type=jnp.float...  30.3 us
    dot_general x1, matrix products, body(): jnp.dot(normed, weight, preferred_element_type=jnp.float32)  28.5 us
    all_gather x1, blocking collectives, body(): normed = lax.all_gather(normed_block, 'dp', axis=0, tiled=True)  15 us
    psum x1, blocking collectives, normalize(): lax.psum((jnp.sum(values, axis=1), jnp.sum(values * values, axis=1)), 'mp')  5.8 us
    ppermute x1, starting transfers between devices, shifted(): lax.ppermute(value, axis, [(i, (i + by) % devices) for i in range(devices)])  2.94 us
    broadcast_in_dim x1, other arithmetic, body(): return result[None]  2.04 us
  transfers between devices with their start and end apart: 2, of which 2 were waited for; matrix products, arithmetic and copies ran while one was open for 1% of the time, Pallas kernels for 0%

commit v1 on v0

v1 whole, which is shorter than its diff:
```python
import functools

import jax
import jax.numpy as jnp
from jax import lax
from jax.experimental import pallas as pl
from jax.experimental.pallas import tpu as pltpu
from jax.sharding import PartitionSpec as P

EPS = 1e-05
LANES = 128
MIB = 1 << 20
VM = pl.BlockSpec(memory_space=pltpu.VMEM)
HB = pl.BlockSpec(memory_space=pl.ANY)
KEPT = 16
PARTS = 4
TILES = 24
SLOTS = 12
FIRST = 7
STEPS = ((0, 8), (6, 12), (12, 18), (16, 21), (21, 24), (24, 24))


def plan(columns):
    if columns % (TILES * LANES) == 0 and columns >= TILES * 512:
        return columns // TILES, SLOTS, FIRST, STEPS
    tile = next(u for u in (256, 128, columns) if columns % u == 0)
    tiles = columns // tile
    return tile, tiles, tiles, ((0, tiles), (tiles - tiles // 2, tiles), (tiles, tiles))


def params(rows):
    return pltpu.CompilerParams(vmem_limit_bytes=(24 if rows > 256 else 8) * MIB)


def cost(flops, read):
    return pl.CostEstimate(flops=int(flops), bytes_accessed=int(read), transcendentals=0)


def fetches(weight, ring, sem, tile, slots, low, high):
    copies = []
    depth = weight.shape[1]
    step = depth // PARTS
    while low < high:
        slot = low % slots
        count = min(high - low, slots - slot)
        for i in range(PARTS):
            rows = pl.ds(i * step, step)
            copies.append(
                pltpu.make_async_copy(
                    weight.at[0, rows, pl.ds(low * tile, count * tile)],
                    ring.at[rows, pl.ds(slot * tile, count * tile)],
                    sem.at[len(copies)],
                )
            )
        low += count
    return copies


def fetch_kernel(tile, slots, first, weight, ring, sem):
    copies = fetches(weight, ring, sem, tile, slots, 0, first)
    for copy in copies:
        copy.start()
    for copy in copies:
        copy.wait()


def fetch(weight, tile, slots, first, rows):
    depth = weight.shape[1]
    return pl.pallas_call(
        functools.partial(fetch_kernel, tile, slots, first),
        out_shape=pltpu.VMEM((depth, slots * tile), weight.dtype),
        in_specs=[HB],
        out_specs=VM,
        scratch_shapes=[pltpu.SemaphoreType.DMA((2 * PARTS,))],
        compiler_params=params(rows),
        cost_estimate=cost(0, depth * first * tile * 2),
        name="fetch",
    )(weight)


def prepare(places, gain, shift, pieces, x_ref, stat_ref):
    rows, width = pieces[0].shape
    tokens = rows * len(pieces)
    gains = gain[...].astype(jnp.float32)
    shifts = shift[...].astype(jnp.float32)
    first = lax.broadcasted_iota(jnp.int32, (16, LANES), 1) < LANES // 2
    for k, piece in enumerate(pieces):
        for sub in range(rows // 16):
            values = piece[pl.ds(sub * 16, 16), :].astype(jnp.float32)
            average = jnp.sum(values, axis=1, keepdims=True) / width
            centred = values - average
            spread = jnp.sum(centred * centred, axis=1, keepdims=True)
            place = pl.ds(pl.multiple_of(places[k] + sub * 16, 16), 16)
            x_ref[place, :] = (centred * gains).astype(jnp.bfloat16)
            stat_ref[place, :] = jnp.where(first, average, spread)
    row = lax.broadcasted_iota(jnp.int32, (16, width), 0)
    extra = jnp.where(row == 0, gains, jnp.where(row == 1, shifts, 0.0))
    x_ref[pl.ds(tokens, 16), :] = extra.astype(jnp.bfloat16)
    rest = x_ref.shape[0] - tokens - 16
    x_ref[pl.ds(tokens + 16, rest), :] = jnp.zeros((rest, width), jnp.bfloat16)


def product(x_ref, ring, tile, slots, index):
    at = pl.ds(pl.multiple_of(lax.rem(index, slots) * tile, tile), tile)
    return jnp.dot(x_ref[...], ring[:, at], preferred_element_type=jnp.float32)


def open_kernel(config, *refs):
    count, direct, tile, slots, low, high, blocks, total = config
    gain, shift = refs[:2]
    pieces = refs[2 : 2 + count]
    _, weight, ring, x_ref, stat_ref, sem = refs[2 + count :]
    copies = fetches(weight, ring, sem, tile, slots, low, high)
    for copy in copies:
        copy.start()

    mine = lax.axis_index("mp")
    size = pieces[0].shape[0]
    block = total // blocks
    owners = list(range(blocks))
    if direct:
        me = lax.axis_index("dp")
        owners = [lax.rem(me + count - k, count) for k in range(count)]
    places = [((o * size // block) ^ mine) * block + (o * size) % block for o in owners]

    @pl.when(mine >= 0)
    def _():
        prepare(places, gain, shift, pieces, x_ref, stat_ref)

    for copy in copies:
        copy.wait()


def raw_kernel(config, x_ref, _, weight, ring, acc_ref, sem):
    tile, slots, low, high = config
    copies = fetches(weight, ring, sem, tile, slots, low, high)
    for copy in copies:
        copy.start()
    rows, width = acc_ref.shape

    @pl.loop(0, width // tile)
    def _(i):
        acc = product(x_ref, ring, tile, slots, i)
        acc_ref[:, pl.ds(pl.multiple_of(i * tile, tile), tile)] = acc[:rows]

    for copy in copies:
        copy.wait()


def merge_kernel(tile, keep, got, *refs):
    kept, away = refs[-2:]
    block = got.shape[0] // 2

    @pl.loop(0, got.shape[1] // tile)
    def _(i):
        at = pl.ds(pl.multiple_of(i * tile, tile), tile)
        total = keep[:, at] + got[:, at].astype(jnp.float32)
        kept[:, at] = total[:block]
        away[:, at] = total[block:].astype(away.dtype)


def merge(keep, got, ring, tile, rows):
    height, width = got.shape[0] // 2, got.shape[1]
    through = [] if ring is None else [ring]
    outs = [pltpu.VMEM(ring.shape, ring.dtype)] if through else []
    outs.append(pltpu.VMEM((height, width), jnp.float32))
    outs.append(pltpu.VMEM((height, width), jnp.bfloat16))
    result = pl.pallas_call(
        functools.partial(merge_kernel, tile),
        out_shape=tuple(outs),
        in_specs=[VM] * (2 + len(through)),
        out_specs=(VM,) * len(outs),
        input_output_aliases={2: 0} if through else {},
        compiler_params=params(rows),
        name="merge",
    )(keep, got, *through)
    return result if through else (None,) + tuple(result)


def coefficients(stats, depth):
    count = len(stats)
    block = stats[0].shape[0] // count

    def parts(lane):
        columns = []
        for j, stat in enumerate(stats):
            whole = stat[:, lane : lane + 1]
            rows = [whole[(b ^ j) * block : ((b ^ j) + 1) * block] for b in range(count)]
            columns.append(jnp.concatenate(rows, axis=0))
        return columns

    averages = parts(0)
    average = sum(averages) / count
    spread = sum(parts(LANES // 2))
    for one in averages:
        spread = spread + depth * (one - average) * (one - average)
    scale = lax.rsqrt(spread / (depth * count) + EPS)
    return scale, averages[0] - average


def activate(bias, low, kept, got, out, start, tile):
    @pl.loop(0, kept.shape[1] // tile)
    def _(i):
        at = pl.multiple_of(i * tile, tile)
        total = kept[:, pl.ds(at, tile)] + got[:, pl.ds(at, tile)].astype(jnp.float32)
        total = total + bias[:, pl.ds(pl.multiple_of(low + at, tile), tile)].astype(jnp.float32)
        result = jax.nn.gelu(total, approximate=True).astype(out.dtype)
        out[:, pl.ds(pl.multiple_of(start + at, tile), tile)] = result


def layer_kernel(config, *refs):
    blocks, depth, tile, slots, base, done, low, high, later, ended, tokens = config
    refs = list(refs)
    take = lambda n: [refs.pop(0) for _ in range(n)]
    x_ref, ring = take(2)
    weight = take(1)[0]
    stats = take(blocks)
    earlier = take(1)[0] if later else None
    bias, kept, got = take(3) if ended is not None else (None,) * 3
    ring = take(1)[0]
    send, keep = take(2)
    out = take(1)[0] if ended is not None else None
    copies = fetches(weight, ring, refs[0], tile, slots, low, high)
    for copy in copies:
        copy.start()
    block = tokens // blocks
    scale, offset = coefficients([s[...] for s in stats], depth)

    def emit(acc, at):
        gains = acc[tokens : tokens + 1]
        shifts = acc[tokens + 1 : tokens + 2]
        values = scale * (acc[:tokens] + offset * gains) + shifts
        for j in range(blocks):
            part = values[j * block : (j + 1) * block]
            place = send if j % 2 else keep
            place[pl.ds((j // 2) * block, block), at] = part.astype(place.dtype)

    start = 0
    if later:
        start = earlier.shape[1]

        @pl.loop(0, start // tile)
        def _(i):
            at = pl.ds(pl.multiple_of(i * tile, tile), tile)
            emit(earlier[:, at], at)

    @pl.loop(0, done - base)
    def _(i):
        acc = product(x_ref, ring, tile, slots, base + i)
        emit(acc, pl.ds(pl.multiple_of(start + i * tile, tile), tile))

    if ended is not None:
        activate(bias, ended, kept, got, out, 0, tile)
    for copy in copies:
        copy.wait()


def layer(x, ring, weight, tile, slots, base, step, stats, earlier, ended, blocks, tokens, low):
    rows = x.shape[0]
    depth = weight.shape[1]
    done, high = step
    args = [x, ring, weight]
    outs = [pltpu.VMEM(ring.shape, ring.dtype)]
    specs = [VM, VM, HB]
    more = list(stats) + ([] if earlier is None else [earlier])
    if ended is not None:
        more += list(ended[1:])
    args += more
    specs += [VM] * len(more)
    width = (done - base) * tile + (0 if earlier is None else earlier.shape[1])
    outs.append(pltpu.VMEM((tokens // 2, width), jnp.bfloat16))
    outs.append(pltpu.VMEM((tokens // 2, width), jnp.float32))
    if ended is not None:
        outs.append(pltpu.VMEM(ended[2].shape, jnp.bfloat16))
    config = (
        blocks,
        depth,
        tile,
        slots,
        base,
        done,
        low,
        high,
        earlier is not None,
        None if ended is None else ended[0],
        tokens,
    )
    read = depth * max(high - low, (done - base) / 2) * tile * 2
    got = list(
        pl.pallas_call(
            functools.partial(layer_kernel, config),
            out_shape=tuple(outs),
            in_specs=specs,
            out_specs=(VM,) * len(outs),
            scratch_shapes=[pltpu.SemaphoreType.DMA((2 * PARTS,))],
            input_output_aliases={1: 0},
            compiler_params=params(rows),
            cost_estimate=cost(2 * rows * depth * (done - base) * tile, read),
            name="layer",
        )(*args)
    )
    return got.pop(0), got


def finale_kernel(config, *refs):
    edges, ready, tile = config
    out = refs[-1].at[0]
    bias = refs[0]
    if ready:
        start, part = refs[1], refs[1]
        width = part.shape[1]
        out[:, pl.ds(0, width)] = part[...]
        refs = refs[1:]
    for g, low in enumerate(edges):
        kept, got = refs[1 + 2 * g], refs[2 + 2 * g]
        activate(bias, low, kept, got, out, low, tile)


def finale(bias, ready, edges, groups, tile, rows):
    args = [bias] + ([] if ready is None else [ready])
    for kept, got in groups:
        args += [kept, got]
    height = groups[0][0].shape[0]
    return pl.pallas_call(
        functools.partial(finale_kernel, (tuple(edges), ready is not None, tile)),
        out_shape=jax.ShapeDtypeStruct((1, height, bias.shape[1]), jnp.bfloat16),
        in_specs=[VM] * len(args),
        out_specs=VM,
        compiler_params=params(rows),
        name="finale",
    )(*args)


def exchange(value, axis, by):
    size = lax.axis_size(axis)
    return lax.ppermute(value, axis, [(i, i ^ by) for i in range(size)])


def gather(block):
    sections, places = lax.axis_size("section"), lax.axis_size("dp")
    if places > 8:
        received = lax.ppermute(
            block, "section", [(s, (s + 1) % sections) for s in range(sections)]
        )
        return [lax.all_gather(received, "dp", axis=0, tiled=True)]
    pieces = []
    for k in range(places):
        pairs = [
            (s * places + d, ((s + 1) % sections) * places + (d + k) % places)
            for s in range(sections)
            for d in range(places)
        ]
        pieces.append(lax.ppermute(block, ("section", "dp"), pairs))
    return pieces


def halved(send, keep, blocks, block):
    by, left = 1, blocks
    width = keep.shape[1]
    while left > 4:
        total = keep + exchange(send, "mp", by).astype(jnp.float32)
        total = total.reshape(left // 4, 2, block, width)
        keep = total[:, 0].reshape(-1, width)
        send = total[:, 1].reshape(-1, width).astype(jnp.bfloat16)
        by, left = by * 2, left // 2
    return keep, exchange(send, "mp", by)


def body(activations, norm_gain, norm_shift, up_weight, up_bias):
    blocks = lax.axis_size("mp")
    tokens = activations.shape[1] * lax.axis_size("dp")
    block = tokens // blocks
    rows = (tokens + 16 + 127) // 128 * 128
    depth = up_weight.shape[1]
    tile, slots, first, steps = plan(up_weight.shape[2])

    pieces = gather(activations[0])
    direct = len(pieces) > 1
    ring = fetch(up_weight, tile, slots, first, rows)
    if not direct:
        pieces = [pieces[0][b * block : (b + 1) * block] for b in range(blocks)]

    _, high = steps[0]
    count = len(pieces)
    config = (count, direct, tile, slots, first, high, blocks, tokens)
    ring, x, stat = pl.pallas_call(
        functools.partial(open_kernel, config),
        out_shape=(
            pltpu.VMEM(ring.shape, ring.dtype),
            pltpu.VMEM((rows, depth), jnp.bfloat16),
            pltpu.VMEM((tokens, LANES), jnp.float32),
        ),
        in_specs=[VM] * (3 + count) + [HB],
        out_specs=(VM,) * 3,
        scratch_shapes=[pltpu.SemaphoreType.DMA((2 * PARTS,))],
        input_output_aliases={2 + count: 0},
        compiler_params=params(rows),
        cost_estimate=cost(10 * tokens * depth, depth * (high - first) * tile * 2),
        name="open",
    )(norm_gain, norm_shift, *pieces, ring, up_weight)
    stats = [stat] + [exchange(stat, "mp", j) for j in range(1, blocks)]

    low = high
    done, high = steps[1]
    ring, earlier = pl.pallas_call(
        functools.partial(raw_kernel, (tile, slots, low, high)),
        out_shape=(
            pltpu.VMEM(ring.shape, ring.dtype),
            pltpu.VMEM((tokens + KEPT, done * tile), jnp.float32),
        ),
        in_specs=[VM, VM, HB],
        out_specs=(VM,) * 2,
        scratch_shapes=[pltpu.SemaphoreType.DMA((2 * PARTS,))],
        input_output_aliases={1: 0},
        compiler_params=params(rows),
        cost_estimate=cost(2 * rows * depth * done * tile, depth * max(high - low, 1) * tile * 2),
        name="raw",
    )(x, ring, up_weight)

    groups = []
    waiting = []
    edges = []
    ready = None
    start = 0

    def join(ring):
        ring, kept, away = merge(*waiting.pop(0), ring, tile, rows)
        groups.append((kept, exchange(away, "mp", blocks // 2)))
        return ring

    last = len(steps) - 3
    for i, step in enumerate(steps[2:]):
        if len(waiting) > 1:
            ring = join(ring)
        ended = (edges[0], up_bias) + groups[0] if i == last and i > 2 else None
        ring, got = layer(
            x, ring, up_weight, tile, slots, done, step, stats, earlier, ended, blocks, tokens, high
        )
        if ended is not None:
            ready = got[2]
        waiting.append(halved(got[0], got[1], blocks, block))
        edges.append(start)
        start += got[0].shape[1]
        earlier = None
        done, high = step
    while waiting:
        join(None)
    if ready is not None:
        groups, edges = groups[1:], edges[1:]
    return finale(up_bias, ready, edges, groups, tile, rows)


def solution(mesh):
    in_specs = (
        P("section", "dp", "mp"),
        P("section", "mp"),
        P("section", "mp"),
        P("section", "mp", "dp"),
        P("section", "dp"),
    )
    out_specs = P("section", "mp", "dp")
    return jax.shard_map(body, mesh=mesh, in_specs=in_specs, out_specs=out_specs, check_vma=False)
```

time: 102 us -> 54.2 us (0.53)
  Pallas kernels: 0 us -> 32 us
  matrix products: 28.5 us -> 0 us
  waiting for transfers between devices: 31.9 us -> 5.53 us
  blocking collectives: 20.8 us -> 0 us
  starting transfers between devices: 2.94 us -> 16.3 us
  between operations: 13.4 us -> 0.18 us
  other arithmetic: 3.8 us -> 0 us
    pallas_call x0 -> x12, Pallas kernels: none -> 32 us  [the longest x4 16.6 us: layer(): pl.pallas_call(functools.partial(layer_kernel, config), out_shape=tuple(o...]
    reduce_scatter x1 -> x0, waiting for transfers between devices: 30.3 us -> none  [body(): lax.psum_scatter(jnp.dot(normed, weight, preferred_element_type=jnp.float...]
    dot_general x1 -> x0, matrix products: 28.5 us -> none  [body(): jnp.dot(normed, weight, preferred_element_type=jnp.float32)]
    all_gather x1 -> x0, blocking collectives: 15 us -> none  [body(): normed = lax.all_gather(normed_block, 'dp', axis=0, tiled=True)]
    ppermute x1 -> x15, starting transfers between devices: 2.94 us -> 16.3 us  [the longest x4 8.42 us: gather(): pieces.append(lax.ppermute(block, ('section', 'dp'), pairs))]
    psum x1 -> x0, blocking collectives: 5.8 us -> none  [normalize(): lax.psum((jnp.sum(values, axis=1), jnp.sum(values * values, axis=1)), 'mp')]
    ppermute x1 -> x15, waiting for transfers between devices: 1.55 us -> 5.53 us  [the longest x11 4.93 us: exchange(): return lax.ppermute(value, axis, [(i, i ^ by) for i in range(size)])]
    broadcast_in_dim x1 -> x0, other arithmetic: 2.04 us -> none  [body(): return result[None]]
  transfers between devices with their start and end apart: 2 -> 15, of which waited for: 2 -> 4; matrix products, arithmetic and copies ran while one was open for 1% -> 0% of each run, Pallas kernels for 0% -> 41%
where the time goes in v1:
time: 54.2 us; the launch traced here: 54.1 us
  Pallas kernels  32 us (59%)
  starting transfers between devices  16.3 us (30%)
  waiting for transfers between devices  5.53 us (10%)
    pallas_call x4, Pallas kernels, layer(): pl.pallas_call(functools.partial(layer_kernel, config), out_shape=tuple(o...  16.6 us
    ppermute x4, starting transfers between devices, gather(): pieces.append(lax.ppermute(block, ('section', 'dp'), pairs))  8.42 us
    ppermute x11, starting transfers between devices, exchange(): return lax.ppermute(value, axis, [(i, i ^ by) for i in range(size)])  7.92 us
    pallas_call x1, Pallas kernels, fetch(): pl.pallas_call(functools.partial(fetch_kernel, tile, slots, first), out_s...  7.39 us
    ppermute x11, waiting for transfers between devices, exchange(): return lax.ppermute(value, axis, [(i, i ^ by) for i in range(size)])  4.93 us
    pallas_call x1, Pallas kernels, body(): pl.pallas_call(functools.partial(raw_kernel, (tile, slots, low, high)), o...  4.74 us
    pallas_call x1, Pallas kernels, body(): pl.pallas_call(functools.partial(open_kernel, config), out_shape=(pltpu.V...  1.93 us
  transfers between devices with their start and end apart: 15, of which 4 were waited for; matrix products, arithmetic and copies ran while one was open for 0% of the time, Pallas kernels for 41%

profile of v1, /device:TPU:0, one launch (start us, length us, event | category | flops | bytes accessed | tf_op | source)
XLA Modules:
  0.0 54.1 jit_solution(2820117174651558943)
XLA Ops:
  0.0 0.0 copy-start.1
  0.0 0.0 copy-start.2
  0.0 6.0 %collective-permute-start.3 = (bf16[16,3072]{1,0:T(8,128)(2,1)}, bf16[16,3072]{1,0:T(8,128)(2,1)S(1)}, u32[]{:S(2)}, u32[]{:S(2)}) collective-permute-start(bf16[16,3072]{1,0:T(8,128)(2,1)} %bitcast.1), channel_id=1, source_target_pairs={{0,28},{4,16},{8,20},{12,24},{16,12},{20,0},{24,4},{28,8},{1,29},{... | collective-permute-start | bytes 294920 | tf_op jit(solution)/shard_map/ppermute | solution.py:353
  6.0 0.0 collective-permute-start.2
  6.0 1.9 %collective-permute-start.1 = (bf16[16,3072]{1,0:T(8,128)(2,1)}, bf16[16,3072]{1,0:T(8,128)(2,1)S(1)}, u32[]{:S(2)}, u32[]{:S(2)}) collective-permute-start(bf16[16,3072]{1,0:T(8,128)(2,1)} %bitcast.3), channel_id=1, source_target_pairs={{0,20},{4,24},{8,28},{12,16},{16,4},{20,8},{24,12},{28,0},{1,21},{... | collective-permute-start | bytes 294920 | tf_op jit(solution)/shard_map/ppermute | solution.py:353
  7.9 0.5 collective-permute-start
  8.4 7.4 %fetch.1.refs_6_ = bf16[3072,6144]{1,0:T(8,128)(2,1)S(1)} custom-call(bf16[1,3072,12288]{2,1,0:T(8,128)(2,1)} %refs_2_.7), custom_call_target="tpu_custom_call" | custom-call | bytes 22020096 | tf_op jit(solution)/shard_map/fetch/pallas_call | solution.py:69
  15.8 0.0 collective-permute-done.3.refs_5_
  15.8 0.0 collective-permute-done.2.refs_4_
  15.9 0.0 collective-permute-done.1.refs_3_
  15.9 0.6 %collective-permute-done.refs_2_ = bf16[16,3072]{1,0:T(8,128)(2,1)S(1)} collective-permute-done((bf16[16,3072]{1,0:T(8,128)(2,1)}, bf16[16,3072]{1,0:T(8,128)(2,1)S(1)}, u32[]{:S(2)}, u32[]{:S(2)}) %collective-permute-start) | collective-permute-done | bytes 98336 | tf_op jit(solution)/shard_map/ppermute | solution.py:353
  16.5 0.0 copy-done.1
  16.5 0.0 copy-done.2
  16.5 1.9 %open.1 = (bf16[3072,6144]{1,0:T(8,128)(2,1)S(1)}, bf16[128,3072]{1,0:T(8,128)(2,1)S(1)}, f32[64,128]{1,0:T(8,128)S(1)}) custom-call(bf16[1,3072]{1,0:T(2,128)(2,1)S(1)} %copy-done.1, bf16[1,3072]{1,0:T(2,128)(2,1)S(1)} %copy-done.2, bf16[16,3072]{1,0:T(8,128)(2,1)S(1)} %collective-permute-done.refs_2_, ...), custom_call_target="tpu_custom_call", output_to_operand_aliasing={{0}: (6, {})} | custom-call | flops 1966080 | bytes 3145728 | tf_op jit(solution)/shard_map/open/pallas_call | solution.py:386
  18.4 0.2 collective-permute-start.6
  18.6 1.4 %collective-permute-start.5 = (f32[64,128]{1,0:T(8,128)S(1)}, f32[64,128]{1,0:T(8,128)S(1)}, u32[]{:S(2)}, u32[]{:S(2)}) collective-permute-start(f32[64,128]{1,0:T(8,128)S(1)} %get-tuple-element.35.refs_3_), channel_id=1, source_target_pairs={{0,2},{1,3},{2,0},{3,1},{4,6},{5,7},{6,4},{7,5},{8,10},{9,11},{10,... | collective-permute-start | bytes 98312 | tf_op jit(solution)/shard_map/ppermute | solution.py:336
  20.1 0.3 collective-permute-start.4
  20.3 4.7 %raw.1 = (bf16[3072,6144]{1,0:T(8,128)(2,1)S(1)}, f32[80,3072]{1,0:T(8,128)S(1)}) custom-call(bf16[128,3072]{1,0:T(8,128)(2,1)S(1)} %get-tuple-element.32.x_ref.refs_0_, bf16[3072,6144]{1,0:T(8,128)(2,1)S(1)} %get-tuple-element.33._, bf16[1,3072,12288]{2,1,0:T(8,128)(2,1)} %refs_2_.7), custom_call_target="tpu_custom_call", output_to_operand_aliasing={{0}: (1, {})} | custom-call | flops 2415919104 | bytes 12582912 | tf_op jit(solution)/shard_map/raw/pallas_call | solution.py:405
  25.1 0.0 collective-permute-done.6.refs_6_
  25.1 0.0 collective-permute-done.5.refs_5_
  25.1 0.0 collective-permute-done.4.refs_4_
  25.1 6.5 %layer.4 = (bf16[3072,6144]{1,0:T(8,128)(2,1)S(1)}, bf16[32,6144]{1,0:T(8,128)(2,1)S(1)}, f32[32,6144]{1,0:T(8,128)S(1)}) custom-call(bf16[128,3072]{1,0:T(8,128)(2,1)S(1)} %get-tuple-element.32.x_ref.refs_0_, bf16[3072,6144]{1,0:T(8,128)(2,1)S(1)} %get-tuple-element.34.refs_1_, bf16[1,3072,12288]{2,1,0:T(8,128)(2,1)} %refs_2_.7, ...), custom_call_target="tpu_custom_call", output_to_operand_aliasing={{0}: (1, {})} | custom-call | flops 2415919104 | bytes 18874368 | tf_op jit(solution)/shard_map/layer/pallas_call | solution.py:290
  31.7 0.3 collective-permute-start.8
  32.0 3.9 %layer.5 = (bf16[3072,6144]{1,0:T(8,128)(2,1)S(1)}, bf16[32,2048]{1,0:T(8,128)(2,1)S(1)}, f32[32,2048]{1,0:T(8,128)S(1)}) custom-call(bf16[128,3072]{1,0:T(8,128)(2,1)S(1)} %get-tuple-element.32.x_ref.refs_0_, bf16[3072,6144]{1,0:T(8,128)(2,1)S(1)} %get-tuple-element.37.refs_1_, bf16[1,3072,12288]{2,1,0:T(8,128)(2,1)} %refs_2_.7, ...), custom_call_target="tpu_custom_call", output_to_operand_aliasing={{0}: (1, {})} | custom-call | flops 1610612736 | bytes 9437184 | tf_op jit(solution)/shard_map/layer/pallas_call | solution.py:290
  35.8 0.0 collective-permute-done.8.got
  35.8 0.1 merge.4
  36.0 1.4 %collective-permute-start.9 = (bf16[16,6144]{1,0:T(8,128)(2,1)S(1)}, bf16[16,6144]{1,0:T(8,128)(2,1)S(1)}, u32[]{:S(2)}, u32[]{:S(2)}) collective-permute-start(bf16[16,6144]{1,0:T(8,128)(2,1)S(1)} %get-tuple-element.47), channel_id=1, source_target_pairs={{0,2},{1,3},{2,0},{3,1},{4,6},{5,7},{6,4},{7,5},{8,10},{9,11},{10,... | collective-permute-start | bytes 589832 | tf_op jit(solution)/shard_map/ppermute | solution.py:336
  37.3 0.2 collective-permute-start.7
  37.6 3.9 %layer.6 = (bf16[3072,6144]{1,0:T(8,128)(2,1)S(1)}, bf16[32,2560]{1,0:T(8,128)(2,1)S(1)}, f32[32,2560]{1,0:T(8,128)S(1)}) custom-call(bf16[128,3072]{1,0:T(8,128)(2,1)S(1)} %get-tuple-element.32.x_ref.refs_0_, bf16[3072,6144]{1,0:T(8,128)(2,1)S(1)} %get-tuple-element.43.refs_1_, bf16[1,3072,12288]{2,1,0:T(8,128)(2,1)} %refs_2_.7, ...), custom_call_target="tpu_custom_call", output_to_operand_aliasing={{0}: (1, {})} | custom-call | flops 2013265920 | bytes 9437184 | tf_op jit(solution)/shard_map/layer/pallas_call | solution.py:290
  41.4 0.0 copy-start
  41.4 0.4 collective-permute-start.11
  41.8 0.0 collective-permute-done.7.got
  41.8 1.3 %collective-permute-done.9.refs_9_ = bf16[16,6144]{1,0:T(8,128)(2,1)S(1)} collective-permute-done((bf16[16,6144]{1,0:T(8,128)(2,1)S(1)}, bf16[16,6144]{1,0:T(8,128)(2,1)S(1)}, u32[]{:S(2)}, u32[]{:S(2)}) %collective-permute-start.9) | collective-permute-done | bytes 196640 | tf_op jit(solution)/shard_map/ppermute | solution.py:336
  43.1 0.0 copy-done
  43.1 2.3 %layer.7 = (bf16[3072,6144]{1,0:T(8,128)(2,1)S(1)}, bf16[32,1536]{1,0:T(8,128)(2,1)S(1)}, f32[32,1536]{1,0:T(8,128)S(1)}, bf16[16,6144]{1,0:T(8,128)(2,1)S(1)}) custom-call(bf16[128,3072]{1,0:T(8,128)(2,1)S(1)} %get-tuple-element.32.x_ref.refs_0_, bf16[3072,6144]{1,0:T(8,128)(2,1)S(1)} %get-tuple-element.45.refs_1_, ...), custom_call_target="tpu_custom_call", output_to_operand_aliasing={{0}: (1, {})} | custom-call | flops 1207959552 | bytes 4718592 | tf_op jit(solution)/shard_map/layer/pallas_call | solution.py:290
  45.5 0.1 collective-permute-start.13
  45.6 0.0 collective-permute-done.11.got
  45.6 0.1 merge.6
  45.6 1.6 %collective-permute-start.12 = (bf16[16,2560]{1,0:T(8,128)(2,1)S(1)}, bf16[16,2560]{1,0:T(8,128)(2,1)S(1)}, u32[]{:S(2)}, u32[]{:S(2)}) collective-permute-start(bf16[16,2560]{1,0:T(8,128)(2,1)S(1)} %get-tuple-element.54), channel_id=1, source_target_pairs={{0,2},{1,3},{2,0},{3,1},{4,6},{5,7},{6,4},{7,5},{8,10},{9,11},{10,... | collective-permute-start | bytes 245768 | tf_op jit(solution)/shard_map/ppermute | solution.py:336
  47.2 0.5 collective-permute-start.10
  47.7 0.0 collective-permute-done.13.got
  47.8 1.6 %collective-permute-start.14 = (bf16[16,1536]{1,0:T(8,128)(2,1)S(1)}, bf16[16,1536]{1,0:T(8,128)(2,1)S(1)}, u32[]{:S(2)}, u32[]{:S(2)}) collective-permute-start(bf16[16,1536]{1,0:T(8,128)(2,1)S(1)} %get-tuple-element.58), channel_id=1, source_target_pairs={{0,2},{1,3},{2,0},{3,1},{4,6},{5,7},{6,4},{7,5},{8,10},{9,11},{10,... | collective-permute-start | bytes 147464 | tf_op jit(solution)/shard_map/ppermute | solution.py:336
  49.3 3.0 %collective-permute-done.10.refs_3_ = bf16[16,2048]{1,0:T(8,128)(2,1)S(1)} collective-permute-done((bf16[16,2048]{1,0:T(8,128)(2,1)S(1)}, bf16[16,2048]{1,0:T(8,128)(2,1)S(1)}, u32[]{:S(2)}, u32[]{:S(2)}) %collective-permute-start.10) | collective-permute-done | bytes 65568 | tf_op jit(solution)/shard_map/ppermute | solution.py:336
  52.3 0.0 collective-permute-done.12.refs_5_
  52.3 0.6 %collective-permute-done.14.refs_7_ = bf16[16,1536]{1,0:T(8,128)(2,1)S(1)} collective-permute-done((bf16[16,1536]{1,0:T(8,128)(2,1)S(1)}, bf16[16,1536]{1,0:T(8,128)(2,1)S(1)}, u32[]{:S(2)}, u32[]{:S(2)}) %collective-permute-start.14) | collective-permute-done | bytes 49184 | tf_op jit(solution)/shard_map/ppermute | solution.py:336
  53.0 1.1 %finale.1 = bf16[1,16,12288]{2,1,0:T(8,128)(2,1)} custom-call(bf16[1,12288]{1,0:T(2,128)(2,1)S(1)} %copy-done, bf16[16,6144]{1,0:T(8,128)(2,1)S(1)} %get-tuple-element.48.refs_1_, f32[16,2048]{1,0:T(8,128)S(1)} %get-tuple-element.49.refs_2_, bf16[16,2048]{1,0:T(8,128)(2,1)S(1)} %collective-permute-done.10.refs_3_, f32[16,2560]{1,0:T(8,128)S(1)} %get-tuple-element.53.refs_4_, ...), custom_call_target="tpu_custom_call" | custom-call | tf_op jit(solution)/shard_map/finale/pallas_call | solution.py:324
  (2 shorter events, 0.1 us)
Async XLA Ops:
  0.0 16.5 %copy-start.1 = (bf16[1,3072]{1,0:T(2,128)(2,1)S(1)}, bf16[1,3072]{1,0:T(2,128)(2,1)}, u32[]{:S(2)}) copy-start(bf16[1,3072]{1,0:T(2,128)(2,1)} %refs_0_.2) | copy-start | bytes 18436
  0.0 16.5 %copy-start.2 = (bf16[1,3072]{1,0:T(2,128)(2,1)S(1)}, bf16[1,3072]{1,0:T(2,128)(2,1)}, u32[]{:S(2)}) copy-start(bf16[1,3072]{1,0:T(2,128)(2,1)} %refs_1_.1) | copy-start | bytes 18436
  0.0 15.8 %collective-permute-start.3 = (bf16[16,3072]{1,0:T(8,128)(2,1)}, bf16[16,3072]{1,0:T(8,128)(2,1)S(1)}, u32[]{:S(2)}, u32[]{:S(2)}) collective-permute-start(bf16[16,3072]{1,0:T(8,128)(2,1)} %bitcast.1), channel_id=1, source_target_pairs={{0,28},{4,16},{8,20},{12,24},{16,12},{20,0},{24,4},{28,8},{1,29},{... | collective-permute-start | bytes 294920 | tf_op jit(solution)/shard_map/ppermute | solution.py:353
  6.0 9.9 %collective-permute-start.2 = (bf16[16,3072]{1,0:T(8,128)(2,1)}, bf16[16,3072]{1,0:T(8,128)(2,1)S(1)}, u32[]{:S(2)}, u32[]{:S(2)}) collective-permute-start(bf16[16,3072]{1,0:T(8,128)(2,1)} %bitcast.2), channel_id=1, source_target_pairs={{0,24},{4,28},{8,16},{12,20},{16,8},{20,12},{24,0},{28,4},{1,25},{... | collective-permute-start | bytes 294920 | tf_op jit(solution)/shard_map/ppermute | solution.py:353
  6.0 9.9 %collective-permute-start.1 = (bf16[16,3072]{1,0:T(8,128)(2,1)}, bf16[16,3072]{1,0:T(8,128)(2,1)S(1)}, u32[]{:S(2)}, u32[]{:S(2)}) collective-permute-start(bf16[16,3072]{1,0:T(8,128)(2,1)} %bitcast.3), channel_id=1, source_target_pairs={{0,20},{4,24},{8,28},{12,16},{16,4},{20,8},{24,12},{28,0},{1,21},{... | collective-permute-start | bytes 294920 | tf_op jit(solution)/shard_map/ppermute | solution.py:353
  7.9 8.6 %collective-permute-start = (bf16[16,3072]{1,0:T(8,128)(2,1)}, bf16[16,3072]{1,0:T(8,128)(2,1)S(1)}, u32[]{:S(2)}, u32[]{:S(2)}) collective-permute-start(bf16[16,3072]{1,0:T(8,128)(2,1)} %bitcast.4), channel_id=1, source_target_pairs={{0,16},{4,20},{8,24},{12,28},{16,0},{20,4},{24,8},{28,12},{1,17},{... | collective-permute-start | bytes 294920 | tf_op jit(solution)/shard_map/ppermute | solution.py:353
  18.4 6.7 %collective-permute-start.6 = (f32[64,128]{1,0:T(8,128)S(1)}, f32[64,128]{1,0:T(8,128)S(1)}, u32[]{:S(2)}, u32[]{:S(2)}) collective-permute-start(f32[64,128]{1,0:T(8,128)S(1)} %get-tuple-element.35.refs_3_), channel_id=1, source_target_pairs={{0,3},{1,2},{2,1},{3,0},{4,7},{5,6},{6,5},{7,4},{8,11},{9,10},{10,... | collective-permute-start | bytes 98312 | tf_op jit(solution)/shard_map/ppermute | solution.py:336
  18.6 6.5 %collective-permute-start.5 = (f32[64,128]{1,0:T(8,128)S(1)}, f32[64,128]{1,0:T(8,128)S(1)}, u32[]{:S(2)}, u32[]{:S(2)}) collective-permute-start(f32[64,128]{1,0:T(8,128)S(1)} %get-tuple-element.35.refs_3_), channel_id=1, source_target_pairs={{0,2},{1,3},{2,0},{3,1},{4,6},{5,7},{6,4},{7,5},{8,10},{9,11},{10,... | collective-permute-start | bytes 98312 | tf_op jit(solution)/shard_map/ppermute | solution.py:336
  20.1 5.0 %collective-permute-start.4 = (f32[64,128]{1,0:T(8,128)S(1)}, f32[64,128]{1,0:T(8,128)S(1)}, u32[]{:S(2)}, u32[]{:S(2)}) collective-permute-start(f32[64,128]{1,0:T(8,128)S(1)} %get-tuple-element.35.refs_3_), channel_id=1, source_target_pairs={{0,1},{1,0},{2,3},{3,2},{4,5},{5,4},{6,7},{7,6},{8,9},{9,8},{10,11... | collective-permute-start | bytes 98312 | tf_op jit(solution)/shard_map/ppermute | solution.py:336
  31.7 4.2 %collective-permute-start.8 = (bf16[32,6144]{1,0:T(8,128)(2,1)S(1)}, bf16[32,6144]{1,0:T(8,128)(2,1)S(1)}, u32[]{:S(2)}, u32[]{:S(2)}) collective-permute-start(bf16[32,6144]{1,0:T(8,128)(2,1)S(1)} %get-tuple-element.41), channel_id=1, source_target_pairs={{0,1},{1,0},{2,3},{3,2},{4,5},{5,4},{6,7},{7,6},{8,9},{9,8},{10,11... | collective-permute-start | bytes 1179656 | tf_op jit(solution)/shard_map/ppermute | solution.py:336
  36.0 7.1 %collective-permute-start.9 = (bf16[16,6144]{1,0:T(8,128)(2,1)S(1)}, bf16[16,6144]{1,0:T(8,128)(2,1)S(1)}, u32[]{:S(2)}, u32[]{:S(2)}) collective-permute-start(bf16[16,6144]{1,0:T(8,128)(2,1)S(1)} %get-tuple-element.47), channel_id=1, source_target_pairs={{0,2},{1,3},{2,0},{3,1},{4,6},{5,7},{6,4},{7,5},{8,10},{9,11},{10,... | collective-permute-start | bytes 589832 | tf_op jit(solution)/shard_map/ppermute | solution.py:336
  37.3 4.5 %collective-permute-start.7 = (bf16[32,2048]{1,0:T(8,128)(2,1)S(1)}, bf16[32,2048]{1,0:T(8,128)(2,1)S(1)}, u32[]{:S(2)}, u32[]{:S(2)}) collective-permute-start(bf16[32,2048]{1,0:T(8,128)(2,1)S(1)} %get-tuple-element.39), channel_id=1, source_target_pairs={{0,1},{1,0},{2,3},{3,2},{4,5},{5,4},{6,7},{7,6},{8,9},{9,8},{10,11... | collective-permute-start | bytes 393224 | tf_op jit(solution)/shard_map/ppermute | solution.py:336
  41.4 1.7 %copy-start = (bf16[1,12288]{1,0:T(2,128)(2,1)S(1)}, bf16[1,12288]{1,0:T(2,128)(2,1)}, u32[]{:S(2)}) copy-start(bf16[1,12288]{1,0:T(2,128)(2,1)} %refs_0_.3) | copy-start | bytes 73732
  41.4 4.1 %collective-permute-start.11 = (bf16[32,2560]{1,0:T(8,128)(2,1)S(1)}, bf16[32,2560]{1,0:T(8,128)(2,1)S(1)}, u32[]{:S(2)}, u32[]{:S(2)}) collective-permute-start(bf16[32,2560]{1,0:T(8,128)(2,1)S(1)} %get-tuple-element.52), channel_id=1, source_target_pairs={{0,1},{1,0},{2,3},{3,2},{4,5},{5,4},{6,7},{7,6},{8,9},{9,8},{10,11... | collective-permute-start | bytes 491528 | tf_op jit(solution)/shard_map/ppermute | solution.py:336
  45.5 2.2 %collective-permute-start.13 = (bf16[32,1536]{1,0:T(8,128)(2,1)S(1)}, bf16[32,1536]{1,0:T(8,128)(2,1)S(1)}, u32[]{:S(2)}, u32[]{:S(2)}) collective-permute-start(bf16[32,1536]{1,0:T(8,128)(2,1)S(1)} %get-tuple-element.56), channel_id=1, source_target_pairs={{0,1},{1,0},{2,3},{3,2},{4,5},{5,4},{6,7},{7,6},{8,9},{9,8},{10,11... | collective-permute-start | bytes 294920 | tf_op jit(solution)/shard_map/ppermute | solution.py:336
  45.6 6.7 %collective-permute-start.12 = (bf16[16,2560]{1,0:T(8,128)(2,1)S(1)}, bf16[16,2560]{1,0:T(8,128)(2,1)S(1)}, u32[]{:S(2)}, u32[]{:S(2)}) collective-permute-start(bf16[16,2560]{1,0:T(8,128)(2,1)S(1)} %get-tuple-element.54), channel_id=1, source_target_pairs={{0,2},{1,3},{2,0},{3,1},{4,6},{5,7},{6,4},{7,5},{8,10},{9,11},{10,... | collective-permute-start | bytes 245768 | tf_op jit(solution)/shard_map/ppermute | solution.py:336
  47.2 5.1 %collective-permute-start.10 = (bf16[16,2048]{1,0:T(8,128)(2,1)S(1)}, bf16[16,2048]{1,0:T(8,128)(2,1)S(1)}, u32[]{:S(2)}, u32[]{:S(2)}) collective-permute-start(bf16[16,2048]{1,0:T(8,128)(2,1)S(1)} %get-tuple-element.50), channel_id=1, source_target_pairs={{0,2},{1,3},{2,0},{3,1},{4,6},{5,7},{6,4},{7,5},{8,10},{9,11},{10,... | collective-permute-start | bytes 196616 | tf_op jit(solution)/shard_map/ppermute | solution.py:336
  47.8 5.2 %collective-permute-start.14 = (bf16[16,1536]{1,0:T(8,128)(2,1)S(1)}, bf16[16,1536]{1,0:T(8,128)(2,1)S(1)}, u32[]{:S(2)}, u32[]{:S(2)}) collective-permute-start(bf16[16,1536]{1,0:T(8,128)(2,1)S(1)} %get-tuple-element.58), channel_id=1, source_target_pairs={{0,2},{1,3},{2,0},{3,1},{4,6},{5,7},{6,4},{7,5},{8,10},{9,11},{10,... | collective-permute-start | bytes 147464 | tf_op jit(solution)/shard_map/ppermute | solution.py:336

commit v2 on v0

v2 whole, which is shorter than its diff:
```python
import functools

import jax
import jax.numpy as jnp
from jax import lax
from jax.experimental import pallas as pl
from jax.experimental.pallas import tpu as pltpu
from jax.sharding import PartitionSpec as P

EPS = 1e-05
LANES = 128
MIB = 1 << 20
VM = pl.BlockSpec(memory_space=pltpu.VMEM)
HB = pl.BlockSpec(memory_space=pl.ANY)
EXTRA = 16
PARTS = 2
PIECE = 2
TILES = 24
SLOTS = 13
FIRST = 8
STEPS = ((8, 13), (20, 20), (24, 24))


def plan(columns):
    if columns % (TILES * LANES) == 0 and columns >= TILES * 512:
        return columns // TILES, SLOTS, FIRST, STEPS
    tile = next(u for u in (256, 128, columns) if columns % u == 0)
    tiles = columns // tile
    return tile, tiles, tiles, ((tiles - tiles // 2, tiles), (tiles, tiles))


def params(rows):
    return pltpu.CompilerParams(vmem_limit_bytes=(24 if rows > 256 else 8) * MIB)


def cost(flops, read):
    return pl.CostEstimate(flops=int(flops), bytes_accessed=int(read), transcendentals=0)


def pieces_of(slots, low, high, size=PIECE):
    result = []
    while low < high:
        count = min(high - low, slots - low % slots, size)
        result.append((low, low + count))
        low += count
    return result


def fetches(weight, ring, sem, tile, slots, pieces):
    step = weight.shape[1] // PARTS
    result = []
    for n, (low, high) in enumerate(pieces):
        columns = (high - low) * tile
        copies = []
        for i in range(PARTS):
            rows = pl.ds(i * step, step)
            copies.append(
                pltpu.make_async_copy(
                    weight.at[0, rows, pl.ds(low * tile, columns)],
                    ring.at[rows, pl.ds(low % slots * tile, columns)],
                    sem.at[n * PARTS + i],
                )
            )
            copies[-1].start()
        result.append(copies)
    return result


def wait(copies):
    for copy in copies:
        copy.wait()


def semaphores(pieces):
    return [pltpu.SemaphoreType.DMA((max(1, len(pieces)) * PARTS,))]


def fetch_kernel(tile, slots, pieces, weight, ring, sem):
    for copies in fetches(weight, ring, sem, tile, slots, pieces):
        wait(copies)


def fetch(weight, tile, slots, first, rows):
    depth = weight.shape[1]
    pieces = pieces_of(slots, 0, first, first)
    return pl.pallas_call(
        functools.partial(fetch_kernel, tile, slots, pieces),
        out_shape=pltpu.VMEM((depth, slots * tile), weight.dtype),
        in_specs=[HB],
        out_specs=VM,
        scratch_shapes=semaphores(pieces),
        compiler_params=params(rows),
        cost_estimate=cost(0, depth * first * tile * 2),
        name="fetch",
    )(weight)


def packed(average, spread):
    lane = lax.broadcasted_iota(jnp.int32, (average.shape[0], LANES), 1)
    return jnp.where(lane < LANES // 2, average, spread)


def unpacked(stat):
    return stat[:, 0:1], stat[:, LANES // 2 : LANES // 2 + 1]


def encoded(average, spread):
    lane = lax.broadcasted_iota(jnp.int32, (average.shape[0], LANES), 1)
    result = jnp.zeros(lane.shape, jnp.float32)
    for base, value in ((0, average), (3, spread)):
        for i in range(3):
            piece = value.astype(jnp.bfloat16).astype(jnp.float32)
            result = jnp.where(lane == base + i, piece, result)
            value = value - piece
    return result.astype(jnp.bfloat16)


def decoded(code):
    values = code.astype(jnp.float32)
    return (
        values[:, 0:1] + values[:, 1:2] + values[:, 2:3],
        values[:, 3:4] + values[:, 4:5] + values[:, 5:6],
    )


def prepare(places, gain, shift, pieces, x_ref, stat_ref):
    rows, width = pieces[0].shape
    tokens = rows * len(pieces)
    gains = gain[...].astype(jnp.float32)
    shifts = shift[...].astype(jnp.float32)
    for k, piece in enumerate(pieces):
        for sub in range(rows // 16):
            values = piece[pl.ds(sub * 16, 16), :].astype(jnp.float32)
            average = jnp.sum(values, axis=1, keepdims=True) / width
            centred = values - average
            spread = jnp.sum(centred * centred, axis=1, keepdims=True)
            place = pl.ds(pl.multiple_of(places[k] + sub * 16, 16), 16)
            x_ref[place, :] = (centred * gains).astype(jnp.bfloat16)
            stat_ref[place, :] = packed(average, spread)
    row = lax.broadcasted_iota(jnp.int32, (EXTRA, width), 0)
    x_ref[pl.ds(tokens, EXTRA), :] = jnp.where(row % 2 == 0, gains, shifts).astype(jnp.bfloat16)
    rest = x_ref.shape[0] - tokens - EXTRA
    x_ref[pl.ds(tokens + EXTRA, rest), :] = jnp.zeros((rest, width), jnp.bfloat16)


def product(x_ref, ring, tile, slots, index):
    at = pl.ds(pl.multiple_of(lax.rem(index, slots) * tile, tile), tile)
    return jnp.dot(x_ref[...], ring[:, at], preferred_element_type=jnp.float32)


def extras(rows):
    high = rows.astype(jnp.bfloat16).astype(jnp.float32)
    return jnp.concatenate([high, rows - high], axis=0).astype(jnp.bfloat16)


def sum_of(code):
    values = code.astype(jnp.float32)
    return values[:8] + values[8:]


def chunk(config, x_ref, ring, stat_ref, outs, coming, fetched):
    blocks, tile, slots, base, done, low, tokens, origin = config
    send, keep, rows, kept_stat = outs
    block = tokens // blocks
    half = tokens // 2
    width = keep.shape[1]

    def multiply(first, last):
        @pl.loop(first, last)
        def _(i):
            acc = product(x_ref, ring, tile, slots, i)
            at = pl.ds(pl.multiple_of((i - origin) * tile, tile), tile)
            for j in range(blocks):
                place = send if j % 2 else keep
                part = acc[j * block : (j + 1) * block]
                place[pl.ds((j // 2) * block, block), at] = part.astype(place.dtype)
            rows[:, at] = acc[tokens : tokens + 8]
            send[pl.ds(half, EXTRA), at] = extras(acc[tokens : tokens + 8])

    multiply(base, min(low, done))
    last = pl.ds(width, LANES)
    for j in range(blocks) if base == origin else ():
        stat = stat_ref[pl.ds(j * block, block), :]
        place = pl.ds((j // 2) * block, block)
        if j % 2:
            send[place, last] = encoded(*unpacked(stat))
        else:
            kept_stat[place, :] = stat
    if base == origin:
        send[pl.ds(half, EXTRA), last] = jnp.zeros((EXTRA, LANES), send.dtype)
    for (first, end), copies in zip(fetched, coming):
        wait(copies)
        if first < done:
            multiply(first, min(end, done))


def open_kernel(config, count, direct, fetched, *refs):
    blocks, total = config[0], config[6]
    tile, slots = config[1:3]
    gain, shift = refs[:2]
    pieces = refs[2 : 2 + count]
    _, weight, ring, x_ref, stat_ref, *outs, sem = refs[2 + count :]
    coming = fetches(weight, ring, sem, tile, slots, fetched)

    mine = lax.axis_index("mp")
    size = pieces[0].shape[0]
    block = total // blocks
    owners = list(range(blocks))
    if direct:
        me = lax.axis_index("dp")
        owners = [lax.rem(me + count - k, count) for k in range(count)]
    places = [((o * size // block) ^ mine) * block + (o * size) % block for o in owners]

    @pl.when(mine >= 0)
    def _():
        prepare(places, gain, shift, pieces, x_ref, stat_ref)

    chunk(config, x_ref, ring, stat_ref, outs, coming, fetched)


def layer_kernel(config, fetched, earlier, x_ref, _, weight, stat_ref, *refs):
    ring = refs[earlier]
    coming = fetches(weight, ring, refs[-1], config[1], config[2], fetched)
    chunk(config, x_ref, ring, stat_ref, refs[-5:-1], coming, fetched)


def outputs(tokens, width):
    half = tokens // 2
    return (
        pltpu.VMEM((half + EXTRA, width + LANES), jnp.bfloat16),
        pltpu.VMEM((half, width), jnp.float32),
        pltpu.VMEM((8, width), jnp.float32),
        pltpu.VMEM((half, LANES), jnp.float32),
    )


def layer(x, ring, weight, stat, config, high, earlier, end):
    blocks, tile, slots, base, done, low, tokens, origin = config
    rows = x.shape[0]
    depth = weight.shape[1]
    fetched = pieces_of(slots, low, high, 1 if done == high else PIECE)
    read = depth * max(high - low, (done - base) / 2) * tile * 2
    return pl.pallas_call(
        functools.partial(layer_kernel, config, fetched, len(earlier)),
        out_shape=(pltpu.VMEM(ring.shape, ring.dtype),) + outputs(tokens, (end - origin) * tile),
        in_specs=[VM, VM, HB, VM] + [VM] * len(earlier),
        out_specs=(VM,) * 5,
        scratch_shapes=semaphores(fetched),
        input_output_aliases={1: 0} | {4 + n: 1 + n for n in range(len(earlier))},
        compiler_params=params(rows),
        cost_estimate=cost(2 * rows * depth * (done - base) * tile, read),
        name="layer",
    )(x, ring, weight, stat, *earlier)


def compact(width):
    return width % (8 * LANES) == 0


def across(column, width):
    high = column.shape[0]
    return jnp.concatenate([jnp.broadcast_to(column, (high, LANES))] * (width // LANES), axis=1)


def stride(widths, tile):
    return next(n * tile for n in (2, 1) if all(width % (n * tile) == 0 for width in widths))


def merge_kernel(config, count, *refs):
    tile, block, features, final = config
    parts = [refs[3 * n : 3 * n + 3] for n in range(count)]
    stat = refs[3 * count]
    kept, rows_out, stat_out, away = refs[-4:]
    high, width = parts[0][0].shape[0], kept.shape[1]
    blocks = high // block
    average, spread = unpacked(stat[...])
    first = parts[0][2]
    other, other_spread = decoded(first[pl.ds(0, high), pl.ds(first.shape[1] - LANES, LANES)])
    apart = average - other
    average = (average + other) / 2
    spread = spread + other_spread + apart * apart * (features / 2)
    folded = final and compact(width)
    tile = stride([keep.shape[1] for keep, _, _ in parts], tile)
    aside = across(apart / 2, tile)

    start = 0
    for keep, rows, got in parts:

        @pl.loop(0, keep.shape[1] // tile)
        def _(i, keep=keep, rows=rows, got=got, start=start):
            at = pl.ds(pl.multiple_of(i * tile, tile), tile)
            to = pl.ds(pl.multiple_of(start + i * tile, tile), tile)
            mine = rows[:, at]
            others = sum_of(got[pl.ds(high, EXTRA), at])
            total = keep[:, at] + got[pl.ds(0, high), at].astype(jnp.float32)
            total = total + aside * (mine[0:1] - others[0:1])
            for k in range(blocks):
                place = away if k % 2 else kept
                part = total[k * block : (k + 1) * block]
                place[pl.ds((k // 2) * block, block), to] = part.astype(place.dtype)
            rows_out[:, to] = mine + others
            if not folded:
                away[pl.ds(high // 2, EXTRA), to] = extras(mine + others)

        start += keep.shape[1]

    last = pl.ds(away.shape[1] - LANES, LANES)
    for k in range(blocks):
        part = slice(k * block, (k + 1) * block)
        place = pl.ds((k // 2) * block, block)
        if k % 2:
            away[place, last] = encoded(average[part], spread[part])
        else:
            stat_out[place, :] = packed(average[part], spread[part])
    if folded:
        fold = width // 8
        lines = [rows_out[r : r + 1, i * fold : (i + 1) * fold] for r in (0, 1) for i in range(8)]
        away[:, pl.ds(width, fold)] = jnp.concatenate(lines, axis=0).astype(away.dtype)
    else:
        away[pl.ds(high // 2, EXTRA), last] = jnp.zeros((EXTRA, LANES), away.dtype)


def merge(parts, stat, ring, tied, config, total):
    tile, block, features, final = config
    half = parts[0][0].shape[0] // 2
    width = sum(keep.shape[1] for keep, _, _ in parts)
    args = [one for part in parts for one in part] + [stat]
    through = [] if ring is None else [ring]
    outs = [pltpu.VMEM(ring.shape, ring.dtype)] if through else []
    outs.append(pltpu.VMEM((half, width), jnp.float32))
    outs.append(pltpu.VMEM((8, width), jnp.float32))
    outs.append(pltpu.VMEM((half, LANES), jnp.float32))
    if final and compact(width):
        outs.append(pltpu.VMEM((half, width + width // 8 + LANES), jnp.bfloat16))
    else:
        outs.append(pltpu.VMEM((half + EXTRA, width + LANES), jnp.bfloat16))
    result = pl.pallas_call(
        functools.partial(merge_kernel, config, len(parts)),
        out_shape=tuple(outs),
        in_specs=[VM] * (len(args) + len(through)) + [HB] * len(tied),
        out_specs=(VM,) * len(outs),
        input_output_aliases={len(args): 0} if through else {},
        compiler_params=params(total),
        name="merge",
    )(*args, *through, *tied)
    ring, result = (result[0], result[1:]) if through else (None, result)
    return ring, result[:3], result[3]


def finish_kernel(config, bias, kept, rows, stat, got, *refs):
    low, tile, features = config
    whole, part, unfolded, sem = refs[-4:]
    height, width = kept.shape
    average, spread = unpacked(stat[...])
    other, other_spread = decoded(got[pl.ds(0, height), pl.ds(got.shape[1] - LANES, LANES)])
    apart = average - other
    spread = spread + other_spread + apart * apart * (features / 2)
    scale = lax.rsqrt(spread / (2 * features) + EPS)
    folded = compact(width)
    tile = stride([width], tile)
    aside = across(apart / 2, tile)
    scale = across(scale, tile)
    if folded:
        fold = width // 8
        code = got[:, pl.ds(width, fold)].astype(jnp.float32)
        for i in range(8):
            unfolded[0:1, i * fold : (i + 1) * fold] = code[i : i + 1]
            unfolded[1:2, i * fold : (i + 1) * fold] = code[8 + i : 9 + i]

    @pl.loop(0, width // tile)
    def _(i):
        at = pl.multiple_of(i * tile, tile)
        here = pl.ds(at, tile)
        mine = rows[:, here]
        others = unfolded[:, here] if folded else sum_of(got[pl.ds(height, EXTRA), here])
        total = kept[:, here] + got[pl.ds(0, height), here].astype(jnp.float32)
        total = total + aside * (mine[0:1] - others[0:1])
        total = scale * total + (mine[1:2] + others[1:2])
        total = total + bias[:, pl.ds(pl.multiple_of(low + at, tile), tile)].astype(jnp.float32)
        part[:, here] = jax.nn.gelu(total, approximate=True).astype(part.dtype)

    copy = pltpu.make_async_copy(part, whole.at[0, :, pl.ds(low, width)], sem)
    copy.start()
    copy.wait()


def finish(bias, low, mine, got, whole, tile, features, total):
    args = [bias, *mine, got] + ([] if whole is None else [whole])
    height, width = mine[0].shape
    return pl.pallas_call(
        functools.partial(finish_kernel, (low, tile, features)),
        out_shape=jax.ShapeDtypeStruct((1, height, bias.shape[1]), jnp.bfloat16),
        in_specs=[VM] * 5 + [HB] * (len(args) - 5),
        out_specs=HB,
        scratch_shapes=[
            pltpu.VMEM((height, width), jnp.bfloat16),
            pltpu.VMEM((8, width), jnp.float32),
            pltpu.SemaphoreType.DMA,
        ],
        input_output_aliases={} if whole is None else {5: 0},
        compiler_params=params(total),
        cost_estimate=cost(20 * height * width, height * width * 8),
        name="finish",
    )(*args)


def exchange(value, axis, by):
    size = lax.axis_size(axis)
    return lax.ppermute(value, axis, [(i, i ^ by) for i in range(size)])


def gather(block):
    sections, places = lax.axis_size("section"), lax.axis_size("dp")
    if places > 8:
        received = lax.ppermute(
            block, "section", [(s, (s + 1) % sections) for s in range(sections)]
        )
        return [lax.all_gather(received, "dp", axis=0, tiled=True)]
    pieces = []
    for k in range(places):
        pairs = [
            (s * places + d, ((s + 1) % sections) * places + (d + k) % places)
            for s in range(sections)
            for d in range(places)
        ]
        pieces.append(lax.ppermute(block, ("section", "dp"), pairs))
    return pieces


def body(activations, norm_gain, norm_shift, up_weight, up_bias):
    blocks = lax.axis_size("mp")
    tokens = activations.shape[1] * lax.axis_size("dp")
    block = tokens // blocks
    rows = (tokens + EXTRA + 127) // 128 * 128
    depth = up_weight.shape[1]
    tile, slots, first, steps = plan(up_weight.shape[2])

    pieces = gather(activations[0])
    direct = len(pieces) > 1
    ring = fetch(up_weight, tile, slots, first, rows)
    if not direct:
        pieces = [pieces[0][b * block : (b + 1) * block] for b in range(blocks)]

    count = len(pieces)
    done, high = steps[0]
    fetched = pieces_of(slots, first, high)
    joint = steps[-2][0] if len(steps) > 2 else done
    config = (blocks, tile, slots, 0, done, first, tokens, 0)
    ring, x, stat, *made = pl.pallas_call(
        functools.partial(open_kernel, config, count, direct, fetched),
        out_shape=(
            pltpu.VMEM(ring.shape, ring.dtype),
            pltpu.VMEM((rows, depth), jnp.bfloat16),
            pltpu.VMEM((tokens, LANES), jnp.float32),
        )
        + outputs(tokens, joint * tile),
        in_specs=[VM] * (3 + count) + [HB],
        out_specs=(VM,) * 7,
        scratch_shapes=semaphores(fetched),
        input_output_aliases={2 + count: 0},
        compiler_params=params(rows),
        cost_estimate=cost(2 * rows * depth * done * tile, depth * max(high - first, 1) * tile * 2),
        name="open",
    )(norm_gain, norm_shift, *pieces, ring, up_weight)

    groups = []
    waiting = []

    def post(made):
        waiting.append((made[1:], exchange(made[0], "mp", 1)))

    def join(ring, start):
        tied = []
        stat = waiting[0][0][2]
        parts = [(keep, lines, got) for (keep, lines, _), got in waiting]
        waiting.clear()
        by = 1
        while 2 * by < blocks:
            config = (tile, block, depth * by, 4 * by == blocks)
            ring, part, away = merge(parts, stat, ring, tied, config, rows)
            by *= 2
            got = exchange(away, "mp", by)
            parts, stat = [(part[0], part[1], got)], part[2]
        groups.append((start, part, got))
        return ring

    for step in steps[1:-1]:
        config = (blocks, tile, slots, done, step[0], high, tokens, 0)
        ring, *made = layer(x, ring, up_weight, stat, config, step[1], made, joint)
        done, high = step
    post(made)
    ring = join(ring, 0)
    config = (blocks, tile, slots, done, steps[-1][0], high, tokens, done)
    ring, *made = layer(x, ring, up_weight, stat, config, steps[-1][1], [], steps[-1][0])
    post(made)
    join(None, done * tile)
    whole = None
    for low, part, got in groups:
        whole = finish(up_bias, low, part, got, whole, tile, depth * blocks // 2, rows)
    return whole


def solution(mesh):
    in_specs = (
        P("section", "dp", "mp"),
        P("section", "mp"),
        P("section", "mp"),
        P("section", "mp", "dp"),
        P("section", "dp"),
    )
    out_specs = P("section", "mp", "dp")
    return jax.shard_map(body, mesh=mesh, in_specs=in_specs, out_specs=out_specs, check_vma=False)
```

time: 102 us -> 48.1 us (0.47)
  Pallas kernels: 0 us -> 30.7 us
  matrix products: 28.5 us -> 0 us
  waiting for transfers between devices: 31.9 us -> 6.37 us
  blocking collectives: 20.8 us -> 0 us
  between operations: 13.4 us -> 0.12 us
  starting transfers between devices: 2.94 us -> 10.7 us
  other arithmetic: 3.8 us -> 0 us
    pallas_call x0 -> x8, Pallas kernels: none -> 30.7 us  [the longest x2 13.6 us: layer(): pl.pallas_call(functools.partial(layer_kernel, config, fetched, len(earli...]
    reduce_scatter x1 -> x0, waiting for transfers between devices: 30.3 us -> none  [body(): lax.psum_scatter(jnp.dot(normed, weight, preferred_element_type=jnp.float...]
    dot_general x1 -> x0, matrix products: 28.5 us -> none  [body(): jnp.dot(normed, weight, preferred_element_type=jnp.float32)]
    all_gather x1 -> x0, blocking collectives: 15 us -> none  [body(): normed = lax.all_gather(normed_block, 'dp', axis=0, tiled=True)]
    ppermute x1 -> x8, starting transfers between devices: 2.94 us -> 10.7 us  [the longest x4 8.42 us: gather(): pieces.append(lax.ppermute(block, ('section', 'dp'), pairs))]
    psum x1 -> x0, blocking collectives: 5.8 us -> none  [normalize(): lax.psum((jnp.sum(values, axis=1), jnp.sum(values * values, axis=1)), 'mp')]
    ppermute x1 -> x8, waiting for transfers between devices: 1.55 us -> 6.37 us  [the longest x4 6.36 us: exchange(): return lax.ppermute(value, axis, [(i, i ^ by) for i in range(size)])]
    broadcast_in_dim x1 -> x0, other arithmetic: 2.04 us -> none  [body(): return result[None]]
  transfers between devices with their start and end apart: 2 -> 8, of which waited for: 2 -> 4; matrix products, arithmetic and copies ran while one was open for 1% -> 0% of each run, Pallas kernels for 0% -> 32%
where the time goes in v2:
time: 48.1 us; the launch traced here: 47.9 us
  Pallas kernels  30.7 us (64%)
  starting transfers between devices  10.7 us (22%)
  waiting for transfers between devices  6.37 us (13%)
    pallas_call x2, Pallas kernels, layer(): pl.pallas_call(functools.partial(layer_kernel, config, fetched, len(earli...  13.6 us
    ppermute x4, starting transfers between devices, gather(): pieces.append(lax.ppermute(block, ('section', 'dp'), pairs))  8.42 us
    pallas_call x1, Pallas kernels, fetch(): pl.pallas_call(functools.partial(fetch_kernel, tile, slots, pieces), out_...  8.17 us
    ppermute x4, waiting for transfers between devices, exchange(): return lax.ppermute(value, axis, [(i, i ^ by) for i in range(size)])  6.36 us
    pallas_call x1, Pallas kernels, body(): pl.pallas_call(functools.partial(open_kernel, config, count, direct, fetc...  5.62 us
    pallas_call x2, Pallas kernels, finish(): pl.pallas_call(functools.partial(finish_kernel, (low, tile, features)), o...  2.5 us
    ppermute x4, starting transfers between devices, exchange(): return lax.ppermute(value, axis, [(i, i ^ by) for i in range(size)])  2.3 us
  transfers between devices with their start and end apart: 8, of which 4 were waited for; matrix products, arithmetic and copies ran while one was open for 0% of the time, Pallas kernels for 32%

profile of v2, /device:TPU:0, one launch (start us, length us, event | category | flops | bytes accessed | tf_op | source)
XLA Modules:
  0.0 47.9 jit_solution(3231659803471746821)
XLA Ops:
  0.0 0.0 copy-start.1
  0.0 0.0 copy-start.2
  0.0 6.0 %collective-permute-start.3 = (bf16[16,3072]{1,0:T(8,128)(2,1)}, bf16[16,3072]{1,0:T(8,128)(2,1)S(1)}, u32[]{:S(2)}, u32[]{:S(2)}) collective-permute-start(bf16[16,3072]{1,0:T(8,128)(2,1)} %bitcast.1), channel_id=1, source_target_pairs={{0,28},{4,16},{8,20},{12,24},{16,12},{20,0},{24,4},{28,8},{1,29},{... | collective-permute-start | bytes 294920 | tf_op jit(solution)/shard_map/ppermute | solution.py:426
  6.0 0.0 collective-permute-start.2
  6.0 1.9 %collective-permute-start.1 = (bf16[16,3072]{1,0:T(8,128)(2,1)}, bf16[16,3072]{1,0:T(8,128)(2,1)S(1)}, u32[]{:S(2)}, u32[]{:S(2)}) collective-permute-start(bf16[16,3072]{1,0:T(8,128)(2,1)} %bitcast.3), channel_id=1, source_target_pairs={{0,20},{4,24},{8,28},{12,16},{16,4},{20,8},{24,12},{28,0},{1,21},{... | collective-permute-start | bytes 294920 | tf_op jit(solution)/shard_map/ppermute | solution.py:426
  7.9 0.5 %collective-permute-start = (bf16[16,3072]{1,0:T(8,128)(2,1)}, bf16[16,3072]{1,0:T(8,128)(2,1)S(1)}, u32[]{:S(2)}, u32[]{:S(2)}) collective-permute-start(bf16[16,3072]{1,0:T(8,128)(2,1)} %bitcast.4), channel_id=1, source_target_pairs={{0,16},{4,20},{8,24},{12,28},{16,0},{20,4},{24,8},{28,12},{1,17},{... | collective-permute-start | bytes 294920 | tf_op jit(solution)/shard_map/ppermute | solution.py:426
  8.4 8.2 %fetch.1.refs_6_ = bf16[3072,6656]{1,0:T(8,128)(2,1)S(1)} custom-call(bf16[1,3072,12288]{2,1,0:T(8,128)(2,1)} %weight.5), custom_call_target="tpu_custom_call" | custom-call | bytes 25165824 | tf_op jit(solution)/shard_map/fetch/pallas_call | solution.py:86
  16.6 0.0 collective-permute-done.3.refs_5_
  16.6 0.0 collective-permute-done.2.refs_4_
  16.6 0.0 collective-permute-done.1.refs_3_
  16.6 0.0 collective-permute-done.refs_2_
  16.7 0.0 copy-done.1
  16.7 0.0 copy-done.2
  16.7 5.6 %open.1 = (bf16[3072,6656]{1,0:T(8,128)(2,1)S(1)}, bf16[128,3072]{1,0:T(8,128)(2,1)S(1)}, f32[64,128]{1,0:T(8,128)S(1)}, bf16[48,10368]{1,0:T(8,128)(2,1)S(1)}, ...) custom-call(bf16[1,3072]{1,0:T(2,128)(2,1)S(1)} %copy-done.1, ...), custom_call_target="tpu_custom_call", output_to_operand_aliasing={{0}: (6, {})} | custom-call | flops 3221225472 | bytes 15728640 | tf_op jit(solution)/shard_map/open/pallas_call | solution.py:449
  22.3 8.2 %layer.2 = (bf16[3072,6656]{1,0:T(8,128)(2,1)S(1)}, bf16[48,10368]{1,0:T(8,128)(2,1)S(1)}, f32[32,10240]{1,0:T(8,128)S(1)}, f32[8,10240]{1,0:T(8,128)S(1)}, f32[32,128]{1,0:T(8,128)S(1)}) custom-call(bf16[128,3072]{1,0:T(8,128)(2,1)S(1)} %get-tuple-element.30.x_ref, ...), custom_call_target="tpu_custom_call", output_to_operand_aliasing={{0}: (1, {}), {1}: (4, {}), {2}: (5, {}), {3}: (6, {}), {4}... | custom-call | flops 4831838208 | bytes 22020096 | tf_op jit(solution)/shard_map/layer/pallas_call | solution.py:243
  30.5 0.1 collective-permute-start.4
  30.6 2.6 %collective-permute-done.4.refs_2_ = bf16[48,10368]{1,0:T(8,128)(2,1)S(1)} collective-permute-done((bf16[48,10368]{1,0:T(8,128)(2,1)S(1)}, bf16[48,10368]{1,0:T(8,128)(2,1)S(1)}, u32[]{:S(2)}, u32[]{:S(2)}) %collective-permute-start.4) | collective-permute-done | bytes 995360 | tf_op jit(solution)/shard_map/ppermute | solution.py:409
  33.2 0.5 %merge.2 = (bf16[3072,6656]{1,0:T(8,128)(2,1)S(1)}, f32[16,10240]{1,0:T(8,128)S(1)}, f32[8,10240]{1,0:T(8,128)S(1)}, f32[16,128]{1,0:T(8,128)S(1)}, bf16[16,11648]{1,0:T(8,128)(2,1)S(1)}) custom-call(f32[32,10240]{1,0:T(8,128)S(1)} %get-tuple-element.37.refs_0_, f32[8,10240]{1,0:T(8,128)S(1)} %get-tuple-element.38.refs_1_, ...), custom_call_target="tpu_custom_call", output_to_operand_aliasing={{0}: (4, {})} | custom-call | tf_op jit(solution)/shard_map/merge/pallas_call | solution.py:337
  33.7 1.6 %collective-permute-start.7 = (bf16[16,11648]{1,0:T(8,128)(2,1)S(1)}, bf16[16,11648]{1,0:T(8,128)(2,1)S(1)}, u32[]{:S(2)}, u32[]{:S(2)}) collective-permute-start(bf16[16,11648]{1,0:T(8,128)(2,1)S(1)} %get-tuple-element.54), channel_id=1, source_target_pairs={{0,2},{1,3},{2,0},{3,1},{4,6},{5,7},{6,4},{7,5},{8,10},{9,11},{10,... | collective-permute-start | bytes 1118216 | tf_op jit(solution)/shard_map/ppermute | solution.py:409
  35.3 0.0 copy-start
  35.3 5.4 %layer.3 = (bf16[3072,6656]{1,0:T(8,128)(2,1)S(1)}, bf16[48,2176]{1,0:T(8,128)(2,1)S(1)}, f32[32,2048]{1,0:T(8,128)S(1)}, f32[8,2048]{1,0:T(8,128)S(1)}, f32[32,128]{1,0:T(8,128)S(1)}) custom-call(bf16[128,3072]{1,0:T(8,128)(2,1)S(1)} %get-tuple-element.30.x_ref, bf16[3072,6656]{1,0:T(8,128)(2,1)S(1)} %get-tuple-element.42._, ...), custom_call_target="tpu_custom_call", output_to_operand_aliasing={{0}: (1, {})} | custom-call | flops 1610612736 | bytes 12582912 | tf_op jit(solution)/shard_map/layer/pallas_call | solution.py:243
  40.7 0.1 collective-permute-start.5
  40.7 1.4 %collective-permute-done.5.refs_2_ = bf16[48,2176]{1,0:T(8,128)(2,1)S(1)} collective-permute-done((bf16[48,2176]{1,0:T(8,128)(2,1)S(1)}, bf16[48,2176]{1,0:T(8,128)(2,1)S(1)}, u32[]{:S(2)}, u32[]{:S(2)}) %collective-permute-start.5) | collective-permute-done | bytes 208928 | tf_op jit(solution)/shard_map/ppermute | solution.py:409
  42.2 0.3 merge.3
  42.5 0.6 %collective-permute-start.6 = (bf16[16,2432]{1,0:T(8,128)(2,1)S(1)}, bf16[16,2432]{1,0:T(8,128)(2,1)S(1)}, u32[]{:S(2)}, u32[]{:S(2)}) collective-permute-start(bf16[16,2432]{1,0:T(8,128)(2,1)S(1)} %get-tuple-element.50), channel_id=1, source_target_pairs={{0,2},{1,3},{2,0},{3,1},{4,6},{5,7},{6,4},{7,5},{8,10},{9,11},{10,... | collective-permute-start | bytes 233480 | tf_op jit(solution)/shard_map/ppermute | solution.py:409
  43.1 1.4 %collective-permute-done.7.got = bf16[16,11648]{1,0:T(8,128)(2,1)S(1)} collective-permute-done((bf16[16,11648]{1,0:T(8,128)(2,1)S(1)}, bf16[16,11648]{1,0:T(8,128)(2,1)S(1)}, u32[]{:S(2)}, u32[]{:S(2)}) %collective-permute-start.7) | collective-permute-done | bytes 372768 | tf_op jit(solution)/shard_map/ppermute | solution.py:409
  44.5 0.0 copy-done
  44.5 1.5 %finish.2.refs_0_ = bf16[1,16,12288]{2,1,0:T(8,128)(2,1)} custom-call(bf16[1,12288]{1,0:T(2,128)(2,1)S(1)} %copy-done, f32[16,10240]{1,0:T(8,128)S(1)} %get-tuple-element.51.kept, f32[8,10240]{1,0:T(8,128)S(1)} %get-tuple-element.52.rows, f32[16,128]{1,0:T(8,128)S(1)} %get-tuple-element.53.stat, bf16[16,11648]{1,0:T(8,128)(2,1)S(1)} %collective-permute-done.7.got), custom_call_target="tpu_custom_call" | custom-call | flops 3276800 | bytes 1310720 | tf_op jit(solution)/shard_map/finish/pallas_call | solution.py:390
  46.0 0.9 %collective-permute-done.6.got = bf16[16,2432]{1,0:T(8,128)(2,1)S(1)} collective-permute-done((bf16[16,2432]{1,0:T(8,128)(2,1)S(1)}, bf16[16,2432]{1,0:T(8,128)(2,1)S(1)}, u32[]{:S(2)}, u32[]{:S(2)}) %collective-permute-start.6) | collective-permute-done | bytes 77856 | tf_op jit(solution)/shard_map/ppermute | solution.py:409
  47.0 1.0 %finish.3 = bf16[1,16,12288]{2,1,0:T(8,128)(2,1)} custom-call(bf16[1,12288]{1,0:T(2,128)(2,1)S(1)} %copy-done, f32[16,2048]{1,0:T(8,128)S(1)} %get-tuple-element.47.kept, f32[8,2048]{1,0:T(8,128)S(1)} %get-tuple-element.48.rows, f32[16,128]{1,0:T(8,128)S(1)} %get-tuple-element.49.stat, ...), custom_call_target="tpu_custom_call", output_to_operand_aliasing={{}: (5, {})} | custom-call | flops 655360 | bytes 262144 | tf_op jit(solution)/shard_map/finish/pallas_call | solution.py:390
Async XLA Ops:
  0.0 16.7 %copy-start.1 = (bf16[1,3072]{1,0:T(2,128)(2,1)S(1)}, bf16[1,3072]{1,0:T(2,128)(2,1)}, u32[]{:S(2)}) copy-start(bf16[1,3072]{1,0:T(2,128)(2,1)} %refs_0_.1) | copy-start | bytes 18436
  0.0 16.7 %copy-start.2 = (bf16[1,3072]{1,0:T(2,128)(2,1)S(1)}, bf16[1,3072]{1,0:T(2,128)(2,1)}, u32[]{:S(2)}) copy-start(bf16[1,3072]{1,0:T(2,128)(2,1)} %refs_1_.1) | copy-start | bytes 18436
  0.0 16.6 %collective-permute-start.3 = (bf16[16,3072]{1,0:T(8,128)(2,1)}, bf16[16,3072]{1,0:T(8,128)(2,1)S(1)}, u32[]{:S(2)}, u32[]{:S(2)}) collective-permute-start(bf16[16,3072]{1,0:T(8,128)(2,1)} %bitcast.1), channel_id=1, source_target_pairs={{0,28},{4,16},{8,20},{12,24},{16,12},{20,0},{24,4},{28,8},{1,29},{... | collective-permute-start | bytes 294920 | tf_op jit(solution)/shard_map/ppermute | solution.py:426
  6.0 10.6 %collective-permute-start.2 = (bf16[16,3072]{1,0:T(8,128)(2,1)}, bf16[16,3072]{1,0:T(8,128)(2,1)S(1)}, u32[]{:S(2)}, u32[]{:S(2)}) collective-permute-start(bf16[16,3072]{1,0:T(8,128)(2,1)} %bitcast.2), channel_id=1, source_target_pairs={{0,24},{4,28},{8,16},{12,20},{16,8},{20,12},{24,0},{28,4},{1,25},{... | collective-permute-start | bytes 294920 | tf_op jit(solution)/shard_map/ppermute | solution.py:426
  6.0 10.6 %collective-permute-start.1 = (bf16[16,3072]{1,0:T(8,128)(2,1)}, bf16[16,3072]{1,0:T(8,128)(2,1)S(1)}, u32[]{:S(2)}, u32[]{:S(2)}) collective-permute-start(bf16[16,3072]{1,0:T(8,128)(2,1)} %bitcast.3), channel_id=1, source_target_pairs={{0,20},{4,24},{8,28},{12,16},{16,4},{20,8},{24,12},{28,0},{1,21},{... | collective-permute-start | bytes 294920 | tf_op jit(solution)/shard_map/ppermute | solution.py:426
  7.9 8.7 %collective-permute-start = (bf16[16,3072]{1,0:T(8,128)(2,1)}, bf16[16,3072]{1,0:T(8,128)(2,1)S(1)}, u32[]{:S(2)}, u32[]{:S(2)}) collective-permute-start(bf16[16,3072]{1,0:T(8,128)(2,1)} %bitcast.4), channel_id=1, source_target_pairs={{0,16},{4,20},{8,24},{12,28},{16,0},{20,4},{24,8},{28,12},{1,17},{... | collective-permute-start | bytes 294920 | tf_op jit(solution)/shard_map/ppermute | solution.py:426
  30.5 2.6 %collective-permute-start.4 = (bf16[48,10368]{1,0:T(8,128)(2,1)S(1)}, bf16[48,10368]{1,0:T(8,128)(2,1)S(1)}, u32[]{:S(2)}, u32[]{:S(2)}) collective-permute-start(bf16[48,10368]{1,0:T(8,128)(2,1)S(1)} %get-tuple-element.39), channel_id=1, source_target_pairs={{0,1},{1,0},{2,3},{3,2},{4,5},{5,4},{6,7},{7,6},{8,9},{9,8},{10,11... | collective-permute-start | bytes 2985992 | tf_op jit(solution)/shard_map/ppermute | solution.py:409
  33.7 10.8 %collective-permute-start.7 = (bf16[16,11648]{1,0:T(8,128)(2,1)S(1)}, bf16[16,11648]{1,0:T(8,128)(2,1)S(1)}, u32[]{:S(2)}, u32[]{:S(2)}) collective-permute-start(bf16[16,11648]{1,0:T(8,128)(2,1)S(1)} %get-tuple-element.54), channel_id=1, source_target_pairs={{0,2},{1,3},{2,0},{3,1},{4,6},{5,7},{6,4},{7,5},{8,10},{9,11},{10,... | collective-permute-start | bytes 1118216 | tf_op jit(solution)/shard_map/ppermute | solution.py:409
  35.3 9.2 %copy-start = (bf16[1,12288]{1,0:T(2,128)(2,1)S(1)}, bf16[1,12288]{1,0:T(2,128)(2,1)}, u32[]{:S(2)}) copy-start(bf16[1,12288]{1,0:T(2,128)(2,1)} %bias.3) | copy-start | bytes 73732
  40.7 1.5 %collective-permute-start.5 = (bf16[48,2176]{1,0:T(8,128)(2,1)S(1)}, bf16[48,2176]{1,0:T(8,128)(2,1)S(1)}, u32[]{:S(2)}, u32[]{:S(2)}) collective-permute-start(bf16[48,2176]{1,0:T(8,128)(2,1)S(1)} %get-tuple-element.45), channel_id=1, source_target_pairs={{0,1},{1,0},{2,3},{3,2},{4,5},{5,4},{6,7},{7,6},{8,9},{9,8},{10,11... | collective-permute-start | bytes 626696 | tf_op jit(solution)/shard_map/ppermute | solution.py:409
  42.5 4.5 %collective-permute-start.6 = (bf16[16,2432]{1,0:T(8,128)(2,1)S(1)}, bf16[16,2432]{1,0:T(8,128)(2,1)S(1)}, u32[]{:S(2)}, u32[]{:S(2)}) collective-permute-start(bf16[16,2432]{1,0:T(8,128)(2,1)S(1)} %get-tuple-element.50), channel_id=1, source_target_pairs={{0,2},{1,3},{2,0},{3,1},{4,6},{5,7},{6,4},{7,5},{8,10},{9,11},{10,... | collective-permute-start | bytes 233480 | tf_op jit(solution)/shard_map/ppermute | solution.py:409
